TPU v7x, 32 devices: a whole 2x2x4 slice. The times are simulated.
32 devices in a mesh: groups: 2 (over y), dom: 4 (over x, core), sub: 4 (over z).
Axes of the slice: x: 2, y: 2, z: 4, core: 2. Of those that a mesh axis runs over, the one named last changes fastest.
Arguments:
- orbitals: float32 [64, 131072], P(None, ('groups', 'dom', 'sub')), parts along dimension 1, may hold values from -6 to 6
- mass_inv: float32 [131072], P(('groups', 'dom', 'sub')), parts along dimension 0, may hold values from 0.5 to 2
- potential: float32 [131072], P(('groups', 'dom', 'sub')), parts along dimension 0, may hold values from -1 to 1
- elem_scale: float32 [4096], P(('groups', 'dom', 'sub')), parts along dimension 0, may hold values from 0.3 to 3
- connectivity: int32 [125, 4096], P(None, ('groups', 'dom', 'sub')), parts along dimension 1, may hold values from 0 to 5631, as said below
- elem_count: int32 [32], P(('groups', 'dom', 'sub')), parts along dimension 0, may hold values from 64 to 128, as said below
- owner_node: int32 [32, 3, 4, 128], P(('groups', 'dom', 'sub')), parts along dimension 0, may hold values from 0 to 4096, as said below
- elem_matrix: float32 [125, 125], replicated
Outputs:
- filtered_one: float32 [64, 131072], P(None, ('groups', 'dom', 'sub')), parts along dimension 1
- filtered_two: float32 [64, 131072], P(None, ('groups', 'dom', 'sub')), parts along dimension 1
There are 2 independent parts, one for each index of `groups`. A program takes and returns all parts, laid end to end along the dimension named above; an argument that names none is the same for every part. Nothing has to cross between parts.
Inputs may be any that keep to these rules, and one draw needn't show every extreme that they name: `elem_count`: some device has exactly 128 elements. `connectivity`: an entry below 4096 names an owned node; an entry 4096 or more names a ghost slot that some owner lists in owner_node. `owner_node`: for each owner, plane q and peer sub index c, the used slots are k below a count of at most 128, the rest hold 4096; some plane of some device uses all 128 slots. Slots toward oneself, toward the plane below dom index 0 and above dom index 3 are unused.
All inputs are finite; a program needn't handle non-finite values.
Results may differ from a plain program's by a relative error of at most 0.0003.
Values sent between devices are 32-bit elements; how exact they have to be, the bound alone decides.
A program may use at most 128 MiB of HBM per device.

v0:
```python
import jax
import jax.numpy as jnp
from jax import lax
from jax.sharding import PartitionSpec as P

shift_center = 0.5
first_gain = 0.8
second_gain = 1.2
memory_gain = 0.5


def with_halo(block, sides, width):
    for axis, dim in sides:
        count = lax.axis_size(axis)
        forward = [(i, i + 1) for i in range(count - 1)]
        backward = [(target, source) for source, target in forward]
        low = lax.ppermute(
            lax.slice_in_dim(block, block.shape[dim] - width, None, axis=dim), axis, forward
        )
        high = lax.ppermute(lax.slice_in_dim(block, 0, width, axis=dim), axis, backward)
        block = jnp.concatenate([low, block, high], axis=dim)
    return block


def keep_planes(extended):
    return jnp.stack([extended[:, 0], extended[:, 2], extended[:, 4]], axis=1)


def on_device(
    orbitals, mass_inv, potential, elem_scale, connectivity, elem_count, owner_node, elem_matrix
):
    orb_rows = orbitals.shape[0]
    owned_total = orbitals.shape[1]
    sub_total = lax.axis_size("sub")
    slot_width = owner_node.shape[3]
    ghost_total = 3 * sub_total * slot_width
    receive = owner_node.reshape(-1)
    elem_total = elem_count[0]
    block_elems = min(128, elem_scale.shape[0])
    block_total = elem_scale.shape[0] // block_elems
    spare_column = jnp.zeros((orb_rows, 1), jnp.float32)

    def to_sharers(values):
        padded = jnp.concatenate([values, spare_column], axis=1)
        outgoing = jnp.take(padded, receive, axis=1).reshape(orb_rows, 3, sub_total, slot_width)
        across = lax.all_to_all(outgoing, "sub", split_axis=2, concat_axis=2, tiled=True)
        arrived = keep_planes(with_halo(across, (("dom", 1),), 1))
        return arrived.reshape(orb_rows, ghost_total)

    def to_owners(local_sums):
        partial_sums = local_sums[:, owned_total:].reshape(orb_rows, 3, sub_total, slot_width)
        across = lax.all_to_all(partial_sums, "sub", split_axis=2, concat_axis=2, tiled=True)
        arrived = keep_planes(with_halo(across, (("dom", 1),), 1))
        owned_pad = jnp.concatenate([local_sums[:, :owned_total], spare_column], axis=1)
        owned_pad = owned_pad.at[:, receive].add(arrived.reshape(orb_rows, ghost_total))
        return owned_pad[:, :owned_total]

    def element_pass(node_table):

        def one_block(block_index, totals):
            begin = block_index * block_elems
            positions = begin + jnp.arange(block_elems, dtype=jnp.int32)
            weight = jnp.where(positions < elem_total, elem_scale, jnp.zeros_like(elem_scale))
            flat = connectivity.reshape(-1)
            gathered = (
                jnp.take(node_table, flat, axis=1).reshape(
                    orb_rows, connectivity.shape[0], block_elems
                )
                * weight
            )
            terms = jnp.einsum(
                "ab,obe->oae", elem_matrix, gathered, precision=lax.Precision.HIGHEST
            )
            return totals.at[:, flat].add(terms.reshape(orb_rows, -1))

        start_sums = jnp.zeros(node_table.shape, jnp.float32)
        return lax.fori_loop(0, block_total, one_block, start_sums)

    def apply_ham(field, ghosts):
        node_table = jnp.concatenate([field, ghosts], axis=1)
        assembled = to_owners(element_pass(node_table))
        return mass_inv * 0.5 * assembled + potential * field

    first = first_gain * (apply_ham(orbitals, to_sharers(orbitals)) - shift_center * orbitals)
    second = (
        second_gain * (apply_ham(first, to_sharers(first)) - shift_center * first)
        - memory_gain * orbitals
    )
    return (first, second)


def solution(mesh):
    placed = (
        P(None, ("groups", "dom", "sub")),
        P(("groups", "dom", "sub")),
        P(("groups", "dom", "sub")),
        P(("groups", "dom", "sub")),
        P(None, ("groups", "dom", "sub")),
        P(("groups", "dom", "sub")),
        P(("groups", "dom", "sub"), None, None, None),
        P(),
    )
    return jax.shard_map(
        on_device,
        mesh=mesh,
        in_specs=placed,
        out_specs=(P(None, ("groups", "dom", "sub")), P(None, ("groups", "dom", "sub"))),
        check_vma=False,
    )
```

profile of v0, /device:TPU:3, one launch (start us, length us, event | category | flops | bytes accessed | tf_op | source)
XLA Modules:
  0.0 495.4 jit_solution(5674858858235892852)
XLA Ops:
  0.6 0.7 reshape.127
  1.4 1.8 copy.51
  3.3 1.6 concatenate.18
  4.8 5.3 %gather_fusion = f32[1536,64]{1,0:T(8,128)} fusion(f32[64,4097]{0,1:T(8,128)} %concatenate.18, s32[2048]{0:T(1024)S(1)} %pad_clamp_fusion.1), kind=kCustom, calls=%fused_computation.clone | custom fusion | bytes 792576 | tf_op jit(solution)/shard_map/jit(_take)/gather | solution.py:45
  10.2 1.4 broadcast_select_fusion.3
  11.6 1.0 copy.49
  12.6 4.6 all-to-all-start
  17.9 10.1 %all-to-all-done = f32[64,3,4,128]{3,0,1,2:T(8,128)S(1)} async-done(((f32[64,3,4,128]{3,0,1,2:T(8,128)}), f32[64,3,4,128]{3,0,1,2:T(8,128)S(1)}, u32[]{:S(2)}, u32[]{:S(2)}) %all-to-all-start) | async-done | bytes 393248 | tf_op jit(solution)/shard_map/all_to_all | solution.py:46
  28.1 1.3 collective-permute-start
  29.4 4.3 collective-permute-start.1
  33.9 0.7 collective-permute-done.1
  34.7 1.2 copy.50
  35.8 2.0 pad_maximum_fusion
  37.9 30.4 %gather_fusion.1 = f32[16000,64]{1,0:T(8,128)} fusion(f32[64,5632]{0,1:T(8,128)S(1)} %pad_maximum_fusion, s32[16384]{0:T(1024)S(1)} %pad_clamp_fusion), kind=kCustom, calls=%fused_computation.1.clone | custom fusion | bytes 8256000 | tf_op jit(solution)/shard_map/while/body/eval_jaxpr/jit(_take)/gather | solution.py:66
  68.3 13.5 %broadcast_select_fusion.1 = f32[16000,64]{1,0:T(8,128)} fusion(f32[16000,64]{1,0:T(8,128)} %gather_fusion.1, pred[16000]{0:T(1024)(128)(4,1)S(1)} %compare_and_fusion), kind=kLoop, calls=%fused_computation.15 | loop fusion | flops 1024000 | bytes 8208000 | tf_op jit(solution)/shard_map/while/body/eval_jaxpr/jit(_take)/select_n | solution.py:66
  81.8 8.9 %copy.52 = f32[64,125,128]{1,2,0:T(8,128)} copy(f32[64,125,128]{0,2,1:T(8,128)} %bitcast.56) | data formatting | bytes 8192000 | tf_op jit(solution)/shard_map/while/body/eval_jaxpr/reshape | solution.py:66
  90.7 6.7 %fusion.4 = f32[64,125,128]{1,2,0:T(8,128)} fusion(f32[64,125,128]{1,2,0:T(8,128)} %copy.52, f32[128]{0:T(128)S(1)} %compare_select_fusion.4, f32[125,125]{1,0:T(8,128)S(1)} %copy-done), kind=kOutput, calls=%fused_computation.18 | convolution fusion | flops 1537024000 | bytes 8255012 | tf_op jit(solution)/shard_map/while/body/eval_jaxpr/ab,obe->oae/dot_general | solution.py:71
  97.5 5.7 %copy.53 = f32[64,125,128]{2,1,0:T(8,128)} copy(f32[64,125,128]{1,2,0:T(8,128)} %fusion.4) | data formatting | bytes 8192000 | tf_op jit(solution)/shard_map/while/body/eval_jaxpr/ab,obe->oae/transpose | solution.py:71
  103.2 6.4 %copy.79 = f32[8,8,125,128]{3,1,2,0:T(8,128)} copy(f32[8,8,125,128]{3,2,1,0:T(8,128)} %bitcast.57) | data formatting | bytes 8192000
  109.6 6.8 %copy.54 = f32[16000,64]{1,0:T(8,128)} copy(f32[16000,64]{0,1:T(8,128)} %bitcast.59) | data formatting | bytes 8192000 | tf_op jit(solution)/shard_map/while/body/eval_jaxpr/reshape | solution.py:74
  116.4 88.7 %scatter_custom_fusion = f32[64,5632]{0,1:T(8,128)S(1)} fusion(s32[16000]{0:T(1024)S(1)} %fusion.25, f32[16000,64]{1,0:T(8,128)} %copy.54, f32[]{:T(128)} %constant.29.clone.1), kind=kCustom, calls=%fused_computation.34 | custom fusion | flops 1024000 | bytes 1442304 | tf_op jit(solution)/shard_map/while/body/eval_jaxpr/scatter-add | solution.py:74
  205.1 0.9 slice.86
  206.0 2.1 copy.55
  208.2 3.5 all-to-all-start.1
  211.7 0.7 broadcast_multiply_fusion
  212.4 6.9 %all-to-all-done.1 = f32[64,3,4,128]{3,0,1,2:T(8,128)S(1)} async-done(((f32[64,3,4,128]{3,0,1,2:T(8,128)}), f32[64,3,4,128]{3,0,1,2:T(8,128)S(1)}, u32[]{:S(2)}, u32[]{:S(2)}) %all-to-all-start.1) | async-done | bytes 393248 | tf_op jit(solution)/shard_map/all_to_all | solution.py:52
  219.4 1.3 collective-permute-start.2
  220.7 7.6 %collective-permute-start.3 = (f32[64,1,4,128]{3,0,1,2:T(8,128)S(1)}, f32[64,1,4,128]{3,0,1,2:T(8,128)S(1)}, u32[]{:S(2)}, u32[]{:S(2)}) collective-permute-start(f32[64,1,4,128]{3,0,1,2:T(8,128)S(1)} %get-tuple-element.67), channel_id=1, source_target_pairs={{4,0},{8,4},{12,8},{5,1},{9,5},{13,9},{6,2},{10,6},{14,10},{7,3},{... | collective-permute-start | bytes 393224 | tf_op jit(solution)/shard_map/ppermute | solution.py:20
  228.3 3.7 slice_select_fusion.1
  232.0 0.3 copy.56
  232.4 0.3 copy.57
  232.7 12.9 %scatter_fusion = f32[64,4097]{0,1:T(8,128)} fusion(f32[64,4097]{0,1:T(8,128)} %slice_select_fusion.1, s32[1536]{0:T(1024)S(1)} %fusion.26, f32[1536,64]{1,0:T(8,128)S(1)} %copy.57), kind=kCustom, calls=%fused_computation.5 | custom fusion | flops 98304 | bytes 1185792 | tf_op jit(solution)/shard_map/scatter-add | solution.py:55
  245.6 3.6 fusion.22
  249.3 1.3 copy-done.4
  250.7 2.6 gather_fusion.2
  253.3 0.3 broadcast_select_fusion.2
  253.6 0.2 copy.60
  253.9 12.8 %all_to_all.20 = f32[64,3,4,128]{3,0,1,2:T(8,128)S(1)} all-to-all(f32[64,3,4,128]{3,0,1,2:T(8,128)S(1)} %copy.60), channel_id=1, replica_groups=mesh['groups'=2,'dom'=4,'sub'=4] {'sub'}, dimensions={2} | all-to-all | bytes 786432 | tf_op jit(solution)/shard_map/all_to_all | solution.py:46
  266.7 1.3 collective-permute-start.4
  268.0 4.8 collective-permute-start.5
  272.8 1.0 collective-permute-done.5
  273.8 1.2 copy.61
  274.9 2.0 pad_maximum_fusion.1
  277.0 30.4 %gather_fusion.3 = f32[16000,64]{1,0:T(8,128)} fusion(f32[64,5632]{0,1:T(8,128)S(1)} %pad_maximum_fusion.1, s32[16384]{0:T(1024)S(1)} %pad_clamp_fusion), kind=kCustom, calls=%fused_computation.3.clone | custom fusion | bytes 8256000 | tf_op jit(solution)/shard_map/while/body/eval_jaxpr/jit(_take)/gather | solution.py:66
  307.4 13.5 %broadcast_select_fusion = f32[16000,64]{1,0:T(8,128)} fusion(f32[16000,64]{1,0:T(8,128)} %gather_fusion.3, pred[16000]{0:T(1024)(128)(4,1)S(1)} %compare_and_fusion), kind=kLoop, calls=%fused_computation.14 | loop fusion | flops 1024000 | bytes 8208000 | tf_op jit(solution)/shard_map/while/body/eval_jaxpr/jit(_take)/select_n | solution.py:66
  320.9 8.9 %copy.62 = f32[64,125,128]{1,2,0:T(8,128)} copy(f32[64,125,128]{0,2,1:T(8,128)} %bitcast.55) | data formatting | bytes 8192000 | tf_op jit(solution)/shard_map/while/body/eval_jaxpr/reshape | solution.py:66
  329.8 6.7 %fusion.7 = f32[64,125,128]{1,2,0:T(8,128)} fusion(f32[64,125,128]{1,2,0:T(8,128)} %copy.62, f32[128]{0:T(128)S(1)} %copy-done.13, f32[125,125]{1,0:T(8,128)S(1)} %copy-done), kind=kOutput, calls=%fused_computation.19 | convolution fusion | flops 1537024000 | bytes 8255012 | tf_op jit(solution)/shard_map/while/body/eval_jaxpr/ab,obe->oae/dot_general | solution.py:71
  336.6 5.7 %copy.63 = f32[64,125,128]{2,1,0:T(8,128)} copy(f32[64,125,128]{1,2,0:T(8,128)} %fusion.7) | data formatting | bytes 8192000 | tf_op jit(solution)/shard_map/while/body/eval_jaxpr/ab,obe->oae/transpose | solution.py:71
  342.3 6.4 %copy.78 = f32[8,8,125,128]{3,1,2,0:T(8,128)} copy(f32[8,8,125,128]{3,2,1,0:T(8,128)} %bitcast.58) | data formatting | bytes 8192000
  348.7 6.8 %copy.64 = f32[16000,64]{1,0:T(8,128)} copy(f32[16000,64]{0,1:T(8,128)} %bitcast.60) | data formatting | bytes 8192000 | tf_op jit(solution)/shard_map/while/body/eval_jaxpr/reshape | solution.py:74
  355.5 89.9 %scatter_custom_fusion.2 = f32[64,5632]{0,1:T(8,128)} fusion(s32[16000]{0:T(1024)S(1)} %fusion.25, f32[16000,64]{1,0:T(8,128)} %copy.64, f32[]{:T(128)} %constant.29.clone.1), kind=kCustom, calls=%fused_computation.32 | custom fusion | flops 1024000 | bytes 1442304 | tf_op jit(solution)/shard_map/while/body/eval_jaxpr/scatter-add | solution.py:74
  445.4 1.2 slice.95
  446.6 1.0 copy.65
  447.6 3.5 all-to-all-start.3
  451.0 1.6 copy.68
  452.6 6.1 %all-to-all-done.3 = f32[64,3,4,128]{3,0,1,2:T(8,128)S(1)} async-done(((f32[64,3,4,128]{3,0,1,2:T(8,128)}), f32[64,3,4,128]{3,0,1,2:T(8,128)S(1)}, u32[]{:S(2)}, u32[]{:S(2)}) %all-to-all-start.3) | async-done | bytes 393248 | tf_op jit(solution)/shard_map/all_to_all | solution.py:52
  458.8 1.3 collective-permute-start.6
  460.1 7.7 %collective-permute-start.7 = (f32[64,1,4,128]{3,0,1,2:T(8,128)S(1)}, f32[64,1,4,128]{3,0,1,2:T(8,128)S(1)}, u32[]{:S(2)}, u32[]{:S(2)}) collective-permute-start(f32[64,1,4,128]{3,0,1,2:T(8,128)S(1)} %get-tuple-element.53), channel_id=1, source_target_pairs={{4,0},{8,4},{12,8},{5,1},{9,5},{13,9},{6,2},{10,6},{14,10},{7,3},{... | collective-permute-start | bytes 393224 | tf_op jit(solution)/shard_map/ppermute | solution.py:20
  467.7 4.7 slice_select_fusion
  472.5 0.3 copy.66
  472.9 0.3 copy.67
  473.2 12.9 %scatter_fusion.1 = f32[64,4097]{0,1:T(8,128)} fusion(f32[64,4097]{0,1:T(8,128)} %slice_select_fusion, s32[1536]{0:T(1024)S(1)} %fusion.26, f32[1536,64]{1,0:T(8,128)S(1)} %copy.67), kind=kCustom, calls=%fused_computation.7 | custom fusion | flops 98304 | bytes 1185792 | tf_op jit(solution)/shard_map/scatter-add | solution.py:55
  486.1 6.1 %fusion.13 = f32[64,4096]{0,1:T(8,128)} fusion(f32[64,4097]{0,1:T(8,128)} %scatter_fusion.1, f32[64,4096]{0,1:T(8,128)S(1)} %copy-done.3, f32[64,4097]{0,1:T(8,128)} %scatter_fusion, f32[4096]{0:T(1024)S(1)} %get-tuple-element.72, f32[4096]{0:T(1024)S(1)} %copy-done.7, f32[4096]{0:T(1024)S(1)} %get-tuple-element.73), kind=kLoop, calls=%fused_computation.26 | loop fusion | flops 3145728 | bytes 4243456 | tf_op jit(solution)/shard_map/sub | solution.py:86
  492.2 3.1 copy.69
  (55 shorter events, 1.0 us)
Async XLA Ops:
  0.6 90.1 %copy-start = (f32[125,125]{1,0:T(8,128)S(1)}, f32[125,125]{1,0:T(8,128)}, u32[]{:S(2)}) copy-start(f32[125,125]{1,0:T(8,128)} %param.19) | copy-start | bytes 187504
  1.4 8.8 %copy-start.10 = (pred[1536]{0:T(1024)(128)(4,1)}, pred[1536]{0:T(1024)(128)(4,1)S(1)}, u32[]{:S(2)}) copy-start(pred[1536]{0:T(1024)(128)(4,1)S(1)} %compare_and_fusion.1) | copy-start | bytes 4612
  3.3 6.9 %copy-start.1 = (f32[64,4096]{0,1:T(8,128)}, f32[64,4096]{0,1:T(8,128)S(1)}, u32[]{:S(2)}) copy-start(f32[64,4096]{0,1:T(8,128)S(1)} %copy.51) | copy-start | bytes 3145732
  4.8 13.0 %copy-start.6 = (s32[125,128]{1,0:T(8,128)S(1)}, s32[125,128]{1,0:T(8,128)}, u32[]{:S(2)}) copy-start(s32[125,128]{1,0:T(8,128)} %param.16) | copy-start | bytes 192004
  4.8 13.0 %copy-start.14 = (f32[128]{0:T(128)S(1)}, f32[128]{0:T(128)}, u32[]{:S(2)}) copy-start(f32[128]{0:T(128)} %param.15) | copy-start | bytes 1540
  12.6 15.5 %all-to-all-start = ((f32[64,3,4,128]{3,0,1,2:T(8,128)}), f32[64,3,4,128]{3,0,1,2:T(8,128)S(1)}, u32[]{:S(2)}, u32[]{:S(2)}) async-start(f32[64,3,4,128]{3,0,1,2:T(8,128)} %copy.49), calls=%async_computation | async-start | bytes 786432 | tf_op jit(solution)/shard_map/all_to_all | solution.py:46
  17.9 72.9 %copy-start.12 = (f32[128]{0:T(128)}, f32[128]{0:T(128)S(1)}, u32[]{:S(2)}) copy-start(f32[128]{0:T(128)S(1)} %compare_select_fusion.4) | copy-start | bytes 1540
  28.1 5.8 %collective-permute-start = (f32[64,1,4,128]{3,0,1,2:T(8,128)S(1)}, f32[64,1,4,128]{3,0,1,2:T(8,128)S(1)}, u32[]{:S(2)}, u32[]{:S(2)}) collective-permute-start(f32[64,1,4,128]{3,0,1,2:T(8,128)S(1)} %get-tuple-element.69), channel_id=1, source_target_pairs={{0,4},{4,8},{8,12},{1,5},{5,9},{9,13},{2,6},{6,10},{10,14},{3,7},{... | collective-permute-start | bytes 393224 | tf_op jit(solution)/shard_map/ppermute | solution.py:17
  29.4 5.3 %collective-permute-start.1 = (f32[64,1,4,128]{3,0,1,2:T(8,128)S(1)}, f32[64,1,4,128]{3,0,1,2:T(8,128)S(1)}, u32[]{:S(2)}, u32[]{:S(2)}) collective-permute-start(f32[64,1,4,128]{3,0,1,2:T(8,128)S(1)} %get-tuple-element.70), channel_id=1, source_target_pairs={{4,0},{8,4},{12,8},{5,1},{9,5},{13,9},{6,2},{10,6},{14,10},{7,3},{... | collective-permute-start | bytes 393224 | tf_op jit(solution)/shard_map/ppermute | solution.py:20
  116.4 95.2 %copy-start.8 = (s32[1,3,4,128]{3,2,1,0:T(4,128)S(1)}, s32[1,3,4,128]{3,2,1,0:T(4,128)}, u32[]{:S(2)}) copy-start(s32[1,3,4,128]{3,2,1,0:T(4,128)} %param.18) | copy-start | bytes 18436
  116.4 95.2 %copy-start.7 = (f32[4096]{0:T(1024)S(1)}, f32[4096]{0:T(1024)}, u32[]{:S(2)}) copy-start(f32[4096]{0:T(1024)} %param.14) | copy-start | bytes 49156
  208.2 11.2 %all-to-all-start.1 = ((f32[64,3,4,128]{3,0,1,2:T(8,128)}), f32[64,3,4,128]{3,0,1,2:T(8,128)S(1)}, u32[]{:S(2)}, u32[]{:S(2)}) async-start(f32[64,3,4,128]{3,0,1,2:T(8,128)} %copy.55), calls=%async_computation.1 | async-start | bytes 786432 | tf_op jit(solution)/shard_map/all_to_all | solution.py:52
  219.4 12.6 %collective-permute-start.2 = (f32[64,1,4,128]{3,0,1,2:T(8,128)S(1)}, f32[64,1,4,128]{3,0,1,2:T(8,128)S(1)}, u32[]{:S(2)}, u32[]{:S(2)}) collective-permute-start(f32[64,1,4,128]{3,0,1,2:T(8,128)S(1)} %get-tuple-element.66), channel_id=1, source_target_pairs={{0,4},{4,8},{8,12},{1,5},{5,9},{9,13},{2,6},{6,10},{10,14},{3,7},{... | collective-permute-start | bytes 393224 | tf_op jit(solution)/shard_map/ppermute | solution.py:17
  220.7 11.3 %collective-permute-start.3 = (f32[64,1,4,128]{3,0,1,2:T(8,128)S(1)}, f32[64,1,4,128]{3,0,1,2:T(8,128)S(1)}, u32[]{:S(2)}, u32[]{:S(2)}) collective-permute-start(f32[64,1,4,128]{3,0,1,2:T(8,128)S(1)} %get-tuple-element.67), channel_id=1, source_target_pairs={{4,0},{8,4},{12,8},{5,1},{9,5},{13,9},{6,2},{10,6},{14,10},{7,3},{... | collective-permute-start | bytes 393224 | tf_op jit(solution)/shard_map/ppermute | solution.py:20
  232.7 12.9 %copy-start.2 = (f32[64,4096]{0,1:T(8,128)S(1)}, f32[64,4096]{0,1:T(8,128)}, u32[]{:S(2)}) copy-start(f32[64,4096]{0,1:T(8,128)} %copy-done.1) | copy-start | bytes 3145732
  249.3 1.3 copy-start.4
  250.6 2.7 copy-start.11
  266.7 6.1 %collective-permute-start.4 = (f32[64,1,4,128]{3,0,1,2:T(8,128)S(1)}, f32[64,1,4,128]{3,0,1,2:T(8,128)S(1)}, u32[]{:S(2)}, u32[]{:S(2)}) collective-permute-start(f32[64,1,4,128]{3,0,1,2:T(8,128)S(1)} %get-tuple-element.55), channel_id=1, source_target_pairs={{0,4},{4,8},{8,12},{1,5},{5,9},{9,13},{2,6},{6,10},{10,14},{3,7},{... | collective-permute-start | bytes 393224 | tf_op jit(solution)/shard_map/ppermute | solution.py:17
  268.0 5.7 %collective-permute-start.5 = (f32[64,1,4,128]{3,0,1,2:T(8,128)S(1)}, f32[64,1,4,128]{3,0,1,2:T(8,128)S(1)}, u32[]{:S(2)}, u32[]{:S(2)}) collective-permute-start(f32[64,1,4,128]{3,0,1,2:T(8,128)S(1)} %get-tuple-element.64), channel_id=1, source_target_pairs={{4,0},{8,4},{12,8},{5,1},{9,5},{13,9},{6,2},{10,6},{14,10},{7,3},{... | collective-permute-start | bytes 393224 | tf_op jit(solution)/shard_map/ppermute | solution.py:20
  320.9 8.9 %copy-start.13 = (f32[128]{0:T(128)S(1)}, f32[128]{0:T(128)}, u32[]{:S(2)}) copy-start(f32[128]{0:T(128)} %copy-done.12) | copy-start | bytes 1540
  355.5 95.5 %copy-start.5 = (f32[64,4096]{0,1:T(8,128)S(1)}, f32[64,4096]{0,1:T(8,128)}, u32[]{:S(2)}) copy-start(f32[64,4096]{0,1:T(8,128)} %copy-done.4) | copy-start | bytes 3145732
  446.6 21.2 %copy-start.9 = (pred[4097]{0:T(1024)(128)(4,1)S(1)}, pred[4097]{0:T(1024)(128)(4,1)}, u32[]{:S(2)}) copy-start(pred[4097]{0:T(1024)(128)(4,1)} %constant.28.clone.1) | copy-start | bytes 12295
  447.6 11.2 %all-to-all-start.3 = ((f32[64,3,4,128]{3,0,1,2:T(8,128)}), f32[64,3,4,128]{3,0,1,2:T(8,128)S(1)}, u32[]{:S(2)}, u32[]{:S(2)}) async-start(f32[64,3,4,128]{3,0,1,2:T(8,128)} %copy.65), calls=%async_computation.3 | async-start | bytes 786432 | tf_op jit(solution)/shard_map/all_to_all | solution.py:52
  458.8 13.7 %collective-permute-start.6 = (f32[64,1,4,128]{3,0,1,2:T(8,128)S(1)}, f32[64,1,4,128]{3,0,1,2:T(8,128)S(1)}, u32[]{:S(2)}, u32[]{:S(2)}) collective-permute-start(f32[64,1,4,128]{3,0,1,2:T(8,128)S(1)} %get-tuple-element.52), channel_id=1, source_target_pairs={{0,4},{4,8},{8,12},{1,5},{5,9},{9,13},{2,6},{6,10},{10,14},{3,7},{... | collective-permute-start | bytes 393224 | tf_op jit(solution)/shard_map/ppermute | solution.py:17
  460.1 12.4 %collective-permute-start.7 = (f32[64,1,4,128]{3,0,1,2:T(8,128)S(1)}, f32[64,1,4,128]{3,0,1,2:T(8,128)S(1)}, u32[]{:S(2)}, u32[]{:S(2)}) collective-permute-start(f32[64,1,4,128]{3,0,1,2:T(8,128)S(1)} %get-tuple-element.53), channel_id=1, source_target_pairs={{4,0},{8,4},{12,8},{5,1},{9,5},{13,9},{6,2},{10,6},{14,10},{7,3},{... | collective-permute-start | bytes 393224 | tf_op jit(solution)/shard_map/ppermute | solution.py:20
  473.2 12.9 %copy-start.3 = (f32[64,4096]{0,1:T(8,128)S(1)}, f32[64,4096]{0,1:T(8,128)}, u32[]{:S(2)}) copy-start(f32[64,4096]{0,1:T(8,128)} %copy-done.1) | copy-start | bytes 3145732
where the time goes:
time: 499 us; the launch traced here: 495 us
  other arithmetic  256 us (51%)
  local copies, waits for them, and re-layouts  145 us (29%)
  starting transfers between devices  41 us (8%)
  waiting for transfers between devices  24.9 us (5%)
  matrix products  13.4 us (3%)
  blocking collectives  12.8 us (3%)
    scatter-add x2, other arithmetic, one_block(): return totals.at[:, flat].add(terms.reshape(orb_rows, -1))  179 us
    gather x2, local copies, waits for them, and re-layouts, one_block(): jnp.take(node_table, flat, axis=1)  60.9 us
    select_n x3, other arithmetic, one_block(): jnp.take(node_table, flat, axis=1)  27 us
    scatter-add x2, other arithmetic, to_owners(): owned_pad.at[:, receive].add(arrived.reshape(orb_rows, ghost_total))  25.8 us
    ppermute x4, starting transfers between devices, with_halo(): lax.ppermute(lax.slice_in_dim(block, 0, width, axis=dim), axis, backward)  24.3 us
    unnamed x35, local copies, waits for them, and re-layouts  20.8 us
    reshape x2, local copies, waits for them, and re-layouts, one_block(): jnp.take(node_table, flat, axis=1)  17.9 us
    reshape x2, local copies, waits for them, and re-layouts, one_block(): return totals.at[:, flat].add(terms.reshape(orb_rows, -1))  13.6 us
  transfers between devices with their start and end apart: 11, of which 5 were waited for; matrix products, arithmetic and copies ran while one was open for 2% of the time, Pallas kernels for 0%

commit v1 on v0

v1 whole, which is shorter than its diff:
```python
import functools

import jax
import jax.numpy as jnp
from jax import lax
from jax.experimental import pallas as pl
from jax.experimental.pallas import tpu as pltpu
from jax.sharding import PartitionSpec as P

shift_center = 0.5
first_gain = 0.8
second_gain = 1.2
memory_gain = 0.5

LANES = 128
MESH = pl.DeviceIdType.MESH
VMEM_LIMIT = 58 * 1024 * 1024
BANKS = 8


def vmem():
    return pl.BlockSpec(memory_space=pltpu.VMEM)


def smem():
    return pl.BlockSpec(memory_space=pltpu.SMEM)


def low_half(shape):
    return lax.broadcasted_iota(jnp.int32, shape, len(shape) - 1) < LANES // 2


def pack_rows(owner_s, table, packed):
    blocks, half = packed.shape[0], packed.shape[1]
    mask = low_half((1, LANES))

    @pl.loop(0, blocks)
    def _(block):
        for k in range(half):
            low = table[pl.ds(owner_s[block, k], 1), :]
            high = table[pl.ds(owner_s[block, half + k], 1), :]
            packed[block, pl.ds(k, 1), :] = jnp.where(mask, low, high)


def start_kernel(owner_s, field, table, packed):
    nodes = field.shape[1]
    for at in range(0, nodes, LANES):
        piece = field[:, at : at + LANES]
        table[at : at + LANES, :] = jnp.concatenate([piece, piece], axis=0).T
    table[nodes:, :] = jnp.zeros((table.shape[0] - nodes, LANES), jnp.float32)
    pack_rows(owner_s, table, packed)


def exchange_kernel(doms, subs, send, recv, send_sem, recv_sem):
    grp = lax.axis_index("groups")
    dom = lax.axis_index("dom")
    sub = lax.axis_index("sub")
    barrier = pltpu.get_barrier_semaphore()

    def each(action):
        for plane in range(3):
            for peer in range(subs):
                there = dom + plane - 1
                live = jnp.logical_and(there >= 0, there < doms)
                if plane == 1:
                    live = jnp.logical_and(live, sub != peer)

                @pl.when(live)
                def _():
                    action(plane, peer, there)

    def greet(plane, peer, there):
        pl.semaphore_signal(
            barrier, inc=1, device_id=(grp, there, peer), device_id_type=MESH
        )

    def copy(plane, peer, there):
        return pltpu.make_async_remote_copy(
            src_ref=send.at[plane * subs + peer],
            dst_ref=recv.at[(2 - plane) * subs + sub],
            send_sem=send_sem.at[plane * subs + peer],
            recv_sem=recv_sem.at[(2 - plane) * subs + sub],
            device_id=(grp, there, peer),
            device_id_type=MESH,
        )

    def arrival(plane, peer, there):
        return pltpu.make_async_remote_copy(
            src_ref=send.at[plane * subs + peer],
            dst_ref=recv.at[plane * subs + peer],
            send_sem=send_sem.at[plane * subs + peer],
            recv_sem=recv_sem.at[plane * subs + peer],
            device_id=(grp, there, peer),
            device_id_type=MESH,
        )

    each(greet)
    planes = jnp.where(dom > 0, 2, 1) + jnp.where(dom < doms - 1, 1, 0)
    pl.semaphore_wait(barrier, planes * subs - 1)
    each(lambda *where: copy(*where).start())
    each(lambda *where: copy(*where).wait_send())
    each(lambda *where: arrival(*where).wait_recv())


def element_kernel(conn_s, table, ghosts, matrix, weight, owned, partial, full, mat, work, *banks):
    nodes = owned.shape[0]
    blocks, half = ghosts.shape[0], ghosts.shape[1]
    rows = matrix.shape[0]
    pairs = conn_s.shape[1] // 2
    mask = low_half((1, LANES))

    mat[...] = jnp.zeros_like(mat)
    mat[:rows, : matrix.shape[1]] = matrix[...]
    full[:nodes, :] = table[:nodes, :]
    for block in range(blocks):
        piece = ghosts[block]
        other = pltpu.roll(piece, LANES // 2, axis=1)
        begin = nodes + block * 2 * half
        wide = low_half(piece.shape)
        full[begin : begin + half, :] = jnp.where(wide, piece, other)
        full[begin + half : begin + 2 * half, :] = jnp.where(wide, other, piece)
    tail = rows - rows % 8
    work[:, tail:, :] = jnp.zeros((pairs, work.shape[1] - tail, LANES), jnp.float32)

    @pl.loop(0, rows)
    def _(j):
        for pair in range(pairs):
            low = full[pl.ds(conn_s[j, 2 * pair], 1), :]
            high = full[pl.ds(conn_s[j, 2 * pair + 1], 1), :]
            work[pair, pl.ds(j, 1), :] = jnp.where(mask, low, high)

    big = mat[...].astype(jnp.bfloat16)
    small = (mat[...] - big.astype(jnp.float32)).astype(jnp.bfloat16)
    step = 4

    @pl.loop(0, pairs // step)
    def _(n):
        piece = jnp.concatenate(
            [work[n * step + k] * weight[n * step + k] for k in range(step)], axis=1
        )
        high = piece.astype(jnp.bfloat16)
        low = (piece - high.astype(jnp.float32)).astype(jnp.bfloat16)
        dot = functools.partial(jnp.dot, preferred_element_type=jnp.float32)
        piece = dot(big, high) + (dot(big, low) + dot(small, high))
        for k in range(step):
            work[n * step + k] = piece[:, k * LANES : (k + 1) * LANES]

    zero = jnp.zeros((8, LANES), jnp.float32)

    @pl.loop(0, full.shape[0] // 64)
    def _(n):
        for bank in banks:
            for r in range(8):
                bank[pl.ds(pl.multiple_of(n * 64 + r * 8, 8), 8), :] = zero

    @pl.loop(0, rows)
    def _(i):
        for pair in range(pairs):
            term = work[pair, pl.ds(i, 1), :]
            for side in range(2):
                bank = banks[(2 * pair + side) % len(banks)]
                at = pl.ds(conn_s[i, 2 * pair + side], 1)
                bank[at, :] = bank[at, :] + term

    def summed(begin, size):
        at = pl.ds(begin, size)
        low = sum([bank[at, :] for bank in banks[2::2]], banks[0][at, :])
        high = sum([bank[at, :] for bank in banks[3::2]], banks[1][at, :])
        both = low_half((size, LANES))
        total = jnp.where(both, low, high)
        return total + pltpu.roll(total, LANES // 2, axis=1)

    @pl.loop(0, nodes // 128)
    def _(n):
        begin = pl.multiple_of(n * 128, 128)
        owned[pl.ds(begin, 128), :] = summed(begin, 128)

    @pl.loop(0, blocks)
    def _(block):
        begin = pl.multiple_of(nodes + block * 2 * half, 64)
        partial[block] = jnp.where(
            low_half((half, LANES)), summed(begin, half), summed(begin + half, half)
        )


def collect(owner_s, arrived, owned, banks):
    nodes = owned.shape[0]
    blocks, half = arrived.shape[0], arrived.shape[1]
    banks[0][:nodes, :] = owned[...]
    for bank in banks[1:]:
        bank[...] = jnp.zeros_like(bank)

    @pl.loop(0, blocks)
    def _(block):
        for k in range(half):
            term = arrived[block, pl.ds(k, 1), :]
            for side in range(2):
                bank = banks[(2 * k + side) % len(banks)]
                at = pl.ds(owner_s[block, side * half + k], 1)
                bank[at, :] = bank[at, :] + term


def assembled_columns(banks, at):
    rows = pl.ds(at, LANES)
    low = sum([bank[rows, :] for bank in banks[2::2]], banks[0][rows, :])
    high = sum([bank[rows, :] for bank in banks[3::2]], banks[1][rows, :])
    both = jnp.where(low_half((LANES, LANES)), low, high).T
    return both[: LANES // 2] + both[LANES // 2 :]


def first_kernel(owner_s, arrived, owned, field, mass, pot, first, table, packed, *banks):
    nodes = field.shape[1]
    collect(owner_s, arrived, owned, banks)
    for at in range(0, nodes, LANES):
        cols = slice(at, at + LANES)
        v = field[:, cols]
        ham = mass[:, cols] * 0.5 * assembled_columns(banks, at) + pot[:, cols] * v
        piece = first_gain * (ham - shift_center * v)
        first[:, cols] = piece
        table[cols, :] = jnp.concatenate([piece, piece], axis=0).T
    table[nodes:, :] = jnp.zeros((table.shape[0] - nodes, LANES), jnp.float32)
    pack_rows(owner_s, table, packed)


def second_kernel(owner_s, arrived, owned, field, older, mass, pot, second, *banks):
    nodes = field.shape[1]
    collect(owner_s, arrived, owned, banks)
    for at in range(0, nodes, LANES):
        cols = slice(at, at + LANES)
        v = field[:, cols]
        ham = mass[:, cols] * 0.5 * assembled_columns(banks, at) + pot[:, cols] * v
        second[:, cols] = second_gain * (ham - shift_center * v) - memory_gain * older[:, cols]


def on_device(
    orbitals, mass_inv, potential, elem_scale, connectivity, elem_count, owner_node, elem_matrix
):
    orbs, nodes = orbitals.shape
    doms = lax.axis_size("dom")
    subs = lax.axis_size("sub")
    cap = owner_node.shape[3]
    elems = elem_scale.shape[0]
    blocks, half = 3 * subs, cap // 2
    rows_up = (elem_matrix.shape[0] + 127) // 128 * 128
    f32 = jnp.float32
    params = pltpu.CompilerParams(vmem_limit_bytes=VMEM_LIMIT)

    owner = owner_node.reshape(blocks, cap)
    mass = mass_inv.reshape(1, nodes)
    pot = potential.reshape(1, nodes)
    weight = jnp.where(jnp.arange(elems, dtype=jnp.int32) < elem_count[0], elem_scale, 0.0)
    weight = jnp.repeat(weight, orbs).reshape(elems // 2, 1, LANES)

    table_shape = jax.ShapeDtypeStruct((nodes + 8, LANES), f32)
    block_shape = jax.ShapeDtypeStruct((blocks, half, LANES), f32)
    field_shape = jax.ShapeDtypeStruct((orbs, nodes), f32)
    owned_shape = jax.ShapeDtypeStruct((nodes, LANES), f32)

    exchange = pl.pallas_call(
        functools.partial(exchange_kernel, doms, subs),
        out_shape=block_shape,
        in_specs=[vmem()],
        out_specs=vmem(),
        scratch_shapes=[
            pltpu.SemaphoreType.DMA((blocks,)),
            pltpu.SemaphoreType.DMA((blocks,)),
        ],
        compiler_params=pltpu.CompilerParams(
            collective_id=0, has_side_effects=True, vmem_limit_bytes=VMEM_LIMIT
        ),
        name="exchange",
    )
    total = nodes + blocks * cap
    element = pl.pallas_call(
        element_kernel,
        out_shape=(owned_shape, block_shape),
        in_specs=[smem(), vmem(), vmem(), vmem(), vmem()],
        out_specs=(vmem(), vmem()),
        scratch_shapes=[
            pltpu.VMEM((total, LANES), f32),
            pltpu.VMEM((rows_up, rows_up), f32),
            pltpu.VMEM((elems // 2, rows_up, LANES), f32),
        ]
        + [pltpu.VMEM((total, LANES), f32)] * BANKS,
        compiler_params=params,
        name="element",
    )
    owner_banks = [pltpu.VMEM((nodes + 8, LANES), f32)] * 4

    table, packed = pl.pallas_call(
        start_kernel,
        out_shape=(table_shape, block_shape),
        in_specs=[smem(), vmem()],
        out_specs=(vmem(), vmem()),
        compiler_params=params,
        name="start",
    )(owner, orbitals)
    owned, partial = element(connectivity, table, exchange(packed), elem_matrix, weight)
    first, table, packed = pl.pallas_call(
        first_kernel,
        out_shape=(field_shape, table_shape, block_shape),
        in_specs=[smem()] + [vmem()] * 5,
        out_specs=(vmem(),) * 3,
        scratch_shapes=owner_banks,
        compiler_params=params,
        name="first",
    )(owner, exchange(partial), owned, orbitals, mass, pot)
    owned, partial = element(connectivity, table, exchange(packed), elem_matrix, weight)
    second = pl.pallas_call(
        second_kernel,
        out_shape=field_shape,
        in_specs=[smem()] + [vmem()] * 6,
        out_specs=vmem(),
        scratch_shapes=owner_banks,
        compiler_params=params,
        name="second",
    )(owner, exchange(partial), owned, first, orbitals, mass, pot)
    return (first, second)


def solution(mesh):
    placed = (
        P(None, ("groups", "dom", "sub")),
        P(("groups", "dom", "sub")),
        P(("groups", "dom", "sub")),
        P(("groups", "dom", "sub")),
        P(None, ("groups", "dom", "sub")),
        P(("groups", "dom", "sub")),
        P(("groups", "dom", "sub"), None, None, None),
        P(),
    )
    return jax.shard_map(
        on_device,
        mesh=mesh,
        in_specs=placed,
        out_specs=(P(None, ("groups", "dom", "sub")), P(None, ("groups", "dom", "sub"))),
        check_vma=False,
    )
```

time: 499 us -> 158 us (0.32)
  other arithmetic: 256 us -> 0.66 us
  Pallas kernels: 0 us -> 153 us
  local copies, waits for them, and re-layouts: 145 us -> 2.28 us
  starting transfers between devices: 41 us -> 0 us
  waiting for transfers between devices: 24.9 us -> 0 us
  matrix products: 13.4 us -> 0 us
  blocking collectives: 12.8 us -> 0 us
    scatter-add x4 -> x0, other arithmetic: 204 us -> none  [the longest x2 179 us: one_block(): return totals.at[:, flat].add(terms.reshape(orb_rows, -1))]
    pallas_call x0 -> x9, Pallas kernels: none -> 153 us  [the longest x2 80.2 us: on_device(): element(connectivity, table, exchange(packed), elem_matrix, weight)]
    gather x4 -> x0, local copies, waits for them, and re-layouts: 68.8 us -> none  [the longest x2 60.9 us: one_block(): jnp.take(node_table, flat, axis=1)]
    reshape x13 -> x1, local copies, waits for them, and re-layouts: 37.4 us -> 1.29 us  [on_device(): owner = owner_node.reshape(blocks, cap)]
    ppermute x8 -> x0, starting transfers between devices: 29.5 us -> none  [the longest x4 24.3 us: with_halo(): lax.ppermute(lax.slice_in_dim(block, 0, width, axis=dim), axis, backward)]
    select_n x9 -> x1, other arithmetic: 29 us -> 0.66 us  [on_device(): jnp.where(jnp.arange(elems, dtype=jnp.int32) < elem_count[0], elem_scale,...]
    all_to_all x3 -> x0, waiting for transfers between devices: 23.2 us -> none  [the longest x2 13 us: to_owners(): lax.all_to_all(partial_sums, 'sub', split_axis=2, concat_axis=2, tiled=True)]
    unnamed x35 -> x0, local copies, waits for them, and re-layouts: 20.8 us -> none
  transfers between devices with their start and end apart: 11 -> 0, of which waited for: 5 -> 0; matrix products, arithmetic and copies ran while one was open for 2% -> 0% of each run, Pallas kernels for 0% -> 0%
where the time goes in v1:
time: 158 us; the launch traced here: 157 us
  Pallas kernels  153 us (97%)
  local copies, waits for them, and re-layouts  2.28 us (1%)
    pallas_call x2, Pallas kernels, on_device(): element(connectivity, table, exchange(packed), elem_matrix, weight)  80.2 us
    pallas_call x2, Pallas kernels, on_device(): exchange(packed)  25.9 us
    pallas_call x2, Pallas kernels, on_device(): exchange(partial)  25.9 us
    pallas_call x1, Pallas kernels, on_device(): pl.pallas_call(first_kernel, out_shape=(field_shape, table_shape, block_s...  9.48 us
    pallas_call x1, Pallas kernels, on_device(): pl.pallas_call(second_kernel, out_shape=field_shape, in_specs=[smem()] +...  7.1 us
    pallas_call x1, Pallas kernels, on_device(): pl.pallas_call(start_kernel, out_shape=(table_shape, block_shape), in_spe...  4.54 us

profile of v1, /device:TPU:3, one launch (start us, length us, event | category | flops | bytes accessed | tf_op | source)
XLA Modules:
  0.0 157.3 jit_solution(12948394455898349817)
XLA Ops:
  1.3 0.7 compare_select_fusion
  1.9 1.3 reshape.20.owner_s
  3.2 0.1 broadcast_in_dim.12
  3.4 0.1 broadcast_in_dim.13
  3.5 0.7 broadcast_in_dim.14.weight
  4.2 4.5 %start.1 = (f32[4104,128]{1,0:T(8,128)}, f32[12,64,128]{2,1,0:T(8,128)}) custom-call(s32[12,128]{1,0:T(8,128)} %reshape.20.owner_s, f32[64,4096]{1,0:T(8,128)} %older.1), custom_call_target="tpu_custom_call" | custom-call | tf_op jit(solution)/shard_map/start/pallas_call | solution.py:290
  8.8 13.7 %exchange.4.ghosts = f32[12,64,128]{2,1,0:T(8,128)} custom-call(f32[12,64,128]{2,1,0:T(8,128)} %get-tuple-element.12.send), custom_call_target="tpu_custom_call" | custom-call | tf_op jit(solution)/shard_map/exchange/pallas_call | solution.py:298
  22.4 40.1 %element.2 = (f32[4096,128]{1,0:T(8,128)}, f32[12,64,128]{2,1,0:T(8,128)}) custom-call(s32[125,128]{1,0:T(8,128)} %conn_s.3, f32[4104,128]{1,0:T(8,128)} %get-tuple-element.11.table, f32[12,64,128]{2,1,0:T(8,128)} %exchange.4.ghosts, f32[125,125]{1,0:T(8,128)} %matrix.3, f32[64,1,128]{2,1,0:T(1,128)} %broadcast_in_dim.14.weight), custom_call_target="tpu_custom_call" | custom-call | tf_op jit(solution)/shard_map/element/pallas_call | solution.py:298
  62.5 13.5 %exchange.5.arrived = f32[12,64,128]{2,1,0:T(8,128)} custom-call(f32[12,64,128]{2,1,0:T(8,128)} %get-tuple-element.13.send), custom_call_target="tpu_custom_call" | custom-call | tf_op jit(solution)/shard_map/exchange/pallas_call | solution.py:307
  76.1 9.5 %first.1 = (f32[64,4096]{1,0:T(8,128)}, f32[4104,128]{1,0:T(8,128)}, f32[12,64,128]{2,1,0:T(8,128)}) custom-call(s32[12,128]{1,0:T(8,128)} %reshape.20.owner_s, f32[12,64,128]{2,1,0:T(8,128)} %exchange.5.arrived, f32[4096,128]{1,0:T(8,128)} %get-tuple-element.14.owned, f32[64,4096]{1,0:T(8,128)} %older.1, f32[1,4096]{1,0:T(1,128)} %bitcast.4, f32[1,4096]{1,0:T(1,128)} %bitcast.6), custom_call_target="tpu_custom_call" | custom-call | tf_op jit(solution)/shard_map/first/pallas_call | solution.py:299
  85.6 12.2 %exchange.6.ghosts = f32[12,64,128]{2,1,0:T(8,128)} custom-call(f32[12,64,128]{2,1,0:T(8,128)} %get-tuple-element.17.send), custom_call_target="tpu_custom_call" | custom-call | tf_op jit(solution)/shard_map/exchange/pallas_call | solution.py:308
  97.8 40.1 %element.3 = (f32[4096,128]{1,0:T(8,128)}, f32[12,64,128]{2,1,0:T(8,128)}) custom-call(s32[125,128]{1,0:T(8,128)} %conn_s.3, f32[4104,128]{1,0:T(8,128)} %get-tuple-element.16.table, f32[12,64,128]{2,1,0:T(8,128)} %exchange.6.ghosts, f32[125,125]{1,0:T(8,128)} %matrix.3, f32[64,1,128]{2,1,0:T(1,128)} %broadcast_in_dim.14.weight), custom_call_target="tpu_custom_call" | custom-call | tf_op jit(solution)/shard_map/element/pallas_call | solution.py:308
  137.9 12.3 %exchange.7.arrived = f32[12,64,128]{2,1,0:T(8,128)} custom-call(f32[12,64,128]{2,1,0:T(8,128)} %get-tuple-element.18.send), custom_call_target="tpu_custom_call" | custom-call | tf_op jit(solution)/shard_map/exchange/pallas_call | solution.py:317
  150.2 7.1 %second.1 = f32[64,4096]{1,0:T(8,128)} custom-call(s32[12,128]{1,0:T(8,128)} %reshape.20.owner_s, f32[12,64,128]{2,1,0:T(8,128)} %exchange.7.arrived, f32[4096,128]{1,0:T(8,128)} %get-tuple-element.19.owned, f32[64,4096]{1,0:T(8,128)} %get-tuple-element.9.field, f32[64,4096]{1,0:T(8,128)} %older.1, f32[1,4096]{1,0:T(1,128)} %bitcast.5, f32[1,4096]{1,0:T(1,128)} %bitcast.7), custom_call_target="tpu_custom_call" | custom-call | tf_op jit(solution)/shard_map/second/pallas_call | solution.py:309

commit v2 on v1

--- a/solution.py
+++ b/solution.py
@@ -30,6 +30,11 @@
     return lax.broadcasted_iota(jnp.int32, shape, len(shape) - 1) < LANES // 2
 
 
+def slot(owner_s, block, k):
+    subs = owner_s.shape[2]
+    return owner_s[0, block // subs, block % subs, k]
+
+
 def pack_rows(owner_s, table, packed):
     blocks, half = packed.shape[0], packed.shape[1]
     mask = low_half((1, LANES))
@@ -37,8 +42,8 @@
     @pl.loop(0, blocks)
     def _(block):
         for k in range(half):
-            low = table[pl.ds(owner_s[block, k], 1), :]
-            high = table[pl.ds(owner_s[block, half + k], 1), :]
+            low = table[pl.ds(slot(owner_s, block, k), 1), :]
+            high = table[pl.ds(slot(owner_s, block, half + k), 1), :]
             packed[block, pl.ds(k, 1), :] = jnp.where(mask, low, high)
 
 
@@ -102,12 +107,28 @@
     each(lambda *where: arrival(*where).wait_recv())
 
 
-def element_kernel(conn_s, table, ghosts, matrix, weight, owned, partial, full, mat, work, *banks):
+def element_kernel(
+    conn, scale_s, count_s, table, ghosts, matrix, owned, partial, full, mat, work, copied, *scratch
+):
     nodes = owned.shape[0]
     blocks, half = ghosts.shape[0], ghosts.shape[1]
     rows = matrix.shape[0]
-    pairs = conn_s.shape[1] // 2
+    pairs = work.shape[0]
+    groups = -(-rows // 8)
+    conn_s, banks = scratch[:groups], scratch[groups:]
     mask = low_half((1, LANES))
+
+    copies = []
+    for group in range(groups):
+        size = min(8, rows - 8 * group)
+        copies.append(
+            pltpu.make_async_copy(
+                conn.at[pl.ds(8 * group, size)],
+                conn_s[group].at[pl.ds(0, size)],
+                copied.at[group],
+            )
+        )
+        copies[-1].start()
 
     mat[...] = jnp.zeros_like(mat)
     mat[:rows, : matrix.shape[1]] = matrix[...]
@@ -121,22 +142,35 @@
         full[begin + half : begin + 2 * half, :] = jnp.where(wide, other, piece)
     tail = rows - rows % 8
     work[:, tail:, :] = jnp.zeros((pairs, work.shape[1] - tail, LANES), jnp.float32)
-
-    @pl.loop(0, rows)
-    def _(j):
-        for pair in range(pairs):
-            low = full[pl.ds(conn_s[j, 2 * pair], 1), :]
-            high = full[pl.ds(conn_s[j, 2 * pair + 1], 1), :]
-            work[pair, pl.ds(j, 1), :] = jnp.where(mask, low, high)
+    for copy in copies:
+        copy.wait()
+
+    zero = jnp.zeros((8, LANES), jnp.float32)
+    share = full.shape[0] // pairs
+
+    @pl.loop(0, pairs)
+    def _(pair):
+        for j in range(rows):
+            low = full[pl.ds(conn_s[j // 8][j % 8, pair], 1), :]
+            high = full[pl.ds(conn_s[j // 8][j % 8, pairs + pair], 1), :]
+            work[pair, j : j + 1, :] = jnp.where(mask, low, high)
+        for bank in banks:
+            for r in range(0, share, 8):
+                bank[pl.ds(pl.multiple_of(pair * share + r, 8), 8), :] = zero
 
     big = mat[...].astype(jnp.bfloat16)
     small = (mat[...] - big.astype(jnp.float32)).astype(jnp.bfloat16)
     step = 4
 
+    def weight(pair):
+        low = jnp.where(pair < count_s[0], scale_s[pair], 0.0)
+        high = jnp.where(pairs + pair < count_s[0], scale_s[pairs + pair], 0.0)
+        return jnp.where(mask, low, high)
+
     @pl.loop(0, pairs // step)
     def _(n):
         piece = jnp.concatenate(
-            [work[n * step + k] * weight[n * step + k] for k in range(step)], axis=1
+            [work[n * step + k] * weight(n * step + k) for k in range(step)], axis=1
         )
         high = piece.astype(jnp.bfloat16)
         low = (piece - high.astype(jnp.float32)).astype(jnp.bfloat16)
@@ -145,49 +179,44 @@
         for k in range(step):
             work[n * step + k] = piece[:, k * LANES : (k + 1) * LANES]
 
-    zero = jnp.zeros((8, LANES), jnp.float32)
-
-    @pl.loop(0, full.shape[0] // 64)
-    def _(n):
-        for bank in banks:
-            for r in range(8):
-                bank[pl.ds(pl.multiple_of(n * 64 + r * 8, 8), 8), :] = zero
-
-    @pl.loop(0, rows)
-    def _(i):
-        for pair in range(pairs):
-            term = work[pair, pl.ds(i, 1), :]
+    @pl.loop(0, pairs)
+    def _(pair):
+        for i in range(rows):
+            term = work[pair, i : i + 1, :]
             for side in range(2):
-                bank = banks[(2 * pair + side) % len(banks)]
-                at = pl.ds(conn_s[i, 2 * pair + side], 1)
+                bank = banks[(2 * i + side) % len(banks)]
+                at = pl.ds(conn_s[i // 8][i % 8, side * pairs + pair], 1)
                 bank[at, :] = bank[at, :] + term
 
     def summed(begin, size):
         at = pl.ds(begin, size)
         low = sum([bank[at, :] for bank in banks[2::2]], banks[0][at, :])
         high = sum([bank[at, :] for bank in banks[3::2]], banks[1][at, :])
-        both = low_half((size, LANES))
-        total = jnp.where(both, low, high)
+        return jnp.where(low_half((size, LANES)), low, high)
+
+    def doubled(begin, size):
+        total = summed(begin, size)
         return total + pltpu.roll(total, LANES // 2, axis=1)
 
-    @pl.loop(0, nodes // 128)
+    @pl.loop(0, nodes // 64)
     def _(n):
-        begin = pl.multiple_of(n * 128, 128)
-        owned[pl.ds(begin, 128), :] = summed(begin, 128)
+        begin = pl.multiple_of(n * 64, 64)
+        owned[pl.ds(begin, 64), :] = summed(begin, 64)
 
     @pl.loop(0, blocks)
     def _(block):
         begin = pl.multiple_of(nodes + block * 2 * half, 64)
         partial[block] = jnp.where(
-            low_half((half, LANES)), summed(begin, half), summed(begin + half, half)
+            low_half((half, LANES)), doubled(begin, half), doubled(begin + half, half)
         )
 
 
 def collect(owner_s, arrived, owned, banks):
     nodes = owned.shape[0]
     blocks, half = arrived.shape[0], arrived.shape[1]
-    banks[0][:nodes, :] = owned[...]
-    for bank in banks[1:]:
+    for bank in banks[:2]:
+        bank[:nodes, :] = owned[...]
+    for bank in banks[2:]:
         bank[...] = jnp.zeros_like(bank)
 
     @pl.loop(0, blocks)
@@ -196,7 +225,7 @@
             term = arrived[block, pl.ds(k, 1), :]
             for side in range(2):
                 bank = banks[(2 * k + side) % len(banks)]
-                at = pl.ds(owner_s[block, side * half + k], 1)
+                at = pl.ds(slot(owner_s, block, side * half + k), 1)
                 bank[at, :] = bank[at, :] + term
 
 
@@ -242,14 +271,13 @@
     elems = elem_scale.shape[0]
     blocks, half = 3 * subs, cap // 2
     rows_up = (elem_matrix.shape[0] + 127) // 128 * 128
+    groups = -(-elem_matrix.shape[0] // 8)
     f32 = jnp.float32
     params = pltpu.CompilerParams(vmem_limit_bytes=VMEM_LIMIT)
 
-    owner = owner_node.reshape(blocks, cap)
+    owner = owner_node
     mass = mass_inv.reshape(1, nodes)
     pot = potential.reshape(1, nodes)
-    weight = jnp.where(jnp.arange(elems, dtype=jnp.int32) < elem_count[0], elem_scale, 0.0)
-    weight = jnp.repeat(weight, orbs).reshape(elems // 2, 1, LANES)
 
     table_shape = jax.ShapeDtypeStruct((nodes + 8, LANES), f32)
     block_shape = jax.ShapeDtypeStruct((blocks, half, LANES), f32)
@@ -274,13 +302,15 @@
     element = pl.pallas_call(
         element_kernel,
         out_shape=(owned_shape, block_shape),
-        in_specs=[smem(), vmem(), vmem(), vmem(), vmem()],
+        in_specs=[pl.BlockSpec(memory_space=pl.ANY), smem(), smem(), vmem(), vmem(), vmem()],
         out_specs=(vmem(), vmem()),
         scratch_shapes=[
             pltpu.VMEM((total, LANES), f32),
             pltpu.VMEM((rows_up, rows_up), f32),
             pltpu.VMEM((elems // 2, rows_up, LANES), f32),
+            pltpu.SemaphoreType.DMA((groups,)),
         ]
+        + [pltpu.SMEM((8, elems), jnp.int32)] * groups
         + [pltpu.VMEM((total, LANES), f32)] * BANKS,
         compiler_params=params,
         name="element",
@@ -295,7 +325,9 @@
         compiler_params=params,
         name="start",
     )(owner, orbitals)
-    owned, partial = element(connectivity, table, exchange(packed), elem_matrix, weight)
+    owned, partial = element(
+        connectivity, elem_scale, elem_count, table, exchange(packed), elem_matrix
+    )
     first, table, packed = pl.pallas_call(
         first_kernel,
         out_shape=(field_shape, table_shape, block_shape),
@@ -305,7 +337,9 @@
         compiler_params=params,
         name="first",
     )(owner, exchange(partial), owned, orbitals, mass, pot)
-    owned, partial = element(connectivity, table, exchange(packed), elem_matrix, weight)
+    owned, partial = element(
+        connectivity, elem_scale, elem_count, table, exchange(packed), elem_matrix
+    )
     second = pl.pallas_call(
         second_kernel,
         out_shape=field_shape,

time: 158 us -> 149 us (0.943)
  Pallas kernels: 153 us -> 147 us
  local copies, waits for them, and re-layouts: 2.28 us -> 0 us
    pallas_call x2, Pallas kernels: 80.2 us -> 73.9 us  [on_device(): element(connectivity, elem_scale, elem_count, table, exchange(packed), el...]
where the time goes in v2:
time: 149 us; the launch traced here: 148 us
  Pallas kernels  147 us (99%)
    pallas_call x2, Pallas kernels, on_device(): element(connectivity, elem_scale, elem_count, table, exchange(packed), el...  73.9 us
    pallas_call x2, Pallas kernels, on_device(): exchange(packed)  26.1 us
    pallas_call x2, Pallas kernels, on_device(): exchange(partial)  25.9 us
    pallas_call x1, Pallas kernels, on_device(): pl.pallas_call(first_kernel, out_shape=(field_shape, table_shape, block_s...  9.43 us
    pallas_call x1, Pallas kernels, on_device(): pl.pallas_call(second_kernel, out_shape=field_shape, in_specs=[smem()] +...  6.97 us
    pallas_call x1, Pallas kernels, on_device(): pl.pallas_call(start_kernel, out_shape=(table_shape, block_shape), in_spe...  4.62 us

profile of v2, /device:TPU:3, one launch (start us, length us, event | category | flops | bytes accessed | tf_op | source)
XLA Modules:
  0.0 148.2 jit_solution(7842250074407871676)
XLA Ops:
  1.3 4.6 %start.1 = (f32[4104,128]{1,0:T(8,128)}, f32[12,64,128]{2,1,0:T(8,128)}) custom-call(s32[1,3,4,128]{3,2,1,0:T(4,128)} %owner_s.5, f32[64,4096]{1,0:T(8,128)} %older.1), custom_call_target="tpu_custom_call" | custom-call | tf_op jit(solution)/shard_map/start/pallas_call | solution.py:320
  5.9 13.7 %exchange.4.ghosts = f32[12,64,128]{2,1,0:T(8,128)} custom-call(f32[12,64,128]{2,1,0:T(8,128)} %get-tuple-element.12.send), custom_call_target="tpu_custom_call" | custom-call | tf_op jit(solution)/shard_map/exchange/pallas_call | solution.py:329
  19.6 37.0 %element.2 = (f32[4096,128]{1,0:T(8,128)}, f32[12,64,128]{2,1,0:T(8,128)}) custom-call(s32[125,128]{1,0:T(8,128)} %conn.3, f32[128]{0:T(128)} %scale_s.3, s32[1]{0:T(128)S(6)} %copy.10.count_s, f32[4104,128]{1,0:T(8,128)} %get-tuple-element.11.table, f32[12,64,128]{2,1,0:T(8,128)} %exchange.4.ghosts, f32[125,125]{1,0:T(8,128)} %matrix.3), custom_call_target="tpu_custom_call" | custom-call | tf_op jit(solution)/shard_map/element/pallas_call | solution.py:328
  56.5 13.6 %exchange.5.arrived = f32[12,64,128]{2,1,0:T(8,128)} custom-call(f32[12,64,128]{2,1,0:T(8,128)} %get-tuple-element.13.send), custom_call_target="tpu_custom_call" | custom-call | tf_op jit(solution)/shard_map/exchange/pallas_call | solution.py:339
  70.1 9.4 %first.1 = (f32[64,4096]{1,0:T(8,128)}, f32[4104,128]{1,0:T(8,128)}, f32[12,64,128]{2,1,0:T(8,128)}) custom-call(s32[1,3,4,128]{3,2,1,0:T(4,128)} %owner_s.5, f32[12,64,128]{2,1,0:T(8,128)} %exchange.5.arrived, f32[4096,128]{1,0:T(8,128)} %get-tuple-element.14.owned, f32[64,4096]{1,0:T(8,128)} %older.1, f32[1,4096]{1,0:T(1,128)} %bitcast.2, f32[1,4096]{1,0:T(1,128)} %bitcast.4), custom_call_target="tpu_custom_call" | custom-call | tf_op jit(solution)/shard_map/first/pallas_call | solution.py:331
  79.5 12.4 %exchange.6.ghosts = f32[12,64,128]{2,1,0:T(8,128)} custom-call(f32[12,64,128]{2,1,0:T(8,128)} %get-tuple-element.17.send), custom_call_target="tpu_custom_call" | custom-call | tf_op jit(solution)/shard_map/exchange/pallas_call | solution.py:341
  92.0 37.0 %element.3 = (f32[4096,128]{1,0:T(8,128)}, f32[12,64,128]{2,1,0:T(8,128)}) custom-call(s32[125,128]{1,0:T(8,128)} %conn.3, f32[128]{0:T(128)} %scale_s.3, s32[1]{0:T(128)S(6)} %copy.10.count_s, f32[4104,128]{1,0:T(8,128)} %get-tuple-element.16.table, f32[12,64,128]{2,1,0:T(8,128)} %exchange.6.ghosts, f32[125,125]{1,0:T(8,128)} %matrix.3), custom_call_target="tpu_custom_call" | custom-call | tf_op jit(solution)/shard_map/element/pallas_call | solution.py:340
  128.9 12.4 %exchange.7.arrived = f32[12,64,128]{2,1,0:T(8,128)} custom-call(f32[12,64,128]{2,1,0:T(8,128)} %get-tuple-element.18.send), custom_call_target="tpu_custom_call" | custom-call | tf_op jit(solution)/shard_map/exchange/pallas_call | solution.py:351
  141.3 7.0 %second.1 = f32[64,4096]{1,0:T(8,128)} custom-call(s32[1,3,4,128]{3,2,1,0:T(4,128)} %owner_s.5, f32[12,64,128]{2,1,0:T(8,128)} %exchange.7.arrived, f32[4096,128]{1,0:T(8,128)} %get-tuple-element.19.owned, f32[64,4096]{1,0:T(8,128)} %get-tuple-element.9.field, f32[64,4096]{1,0:T(8,128)} %older.1, f32[1,4096]{1,0:T(1,128)} %bitcast.3, f32[1,4096]{1,0:T(1,128)} %bitcast.5), custom_call_target="tpu_custom_call" | custom-call | tf_op jit(solution)/shard_map/second/pallas_call | solution.py:343

commit v3 on v2

--- a/solution.py
+++ b/solution.py
@@ -16,6 +16,7 @@
 MESH = pl.DeviceIdType.MESH
 VMEM_LIMIT = 58 * 1024 * 1024
 BANKS = 8
+GROUP = 2
 
 
 def vmem():
@@ -108,22 +109,23 @@
 
 
 def element_kernel(
-    conn, scale_s, count_s, table, ghosts, matrix, owned, partial, full, mat, work, copied, *scratch
+    conn, scale_s, count_s, table, ghosts, matrix, owned, partial, full, mat, copied, *scratch
 ):
     nodes = owned.shape[0]
     blocks, half = ghosts.shape[0], ghosts.shape[1]
     rows = matrix.shape[0]
-    pairs = work.shape[0]
-    groups = -(-rows // 8)
-    conn_s, banks = scratch[:groups], scratch[groups:]
+    pairs = conn.shape[1] // 2
+    groups = -(-rows // GROUP)
+    conn_s, inputs = scratch[:groups], scratch[groups : groups + 2]
+    terms, banks = scratch[groups + 2 : groups + 4], scratch[groups + 4 :]
     mask = low_half((1, LANES))
 
     copies = []
     for group in range(groups):
-        size = min(8, rows - 8 * group)
+        size = min(GROUP, rows - GROUP * group)
         copies.append(
             pltpu.make_async_copy(
-                conn.at[pl.ds(8 * group, size)],
+                conn.at[pl.ds(GROUP * group, size)],
                 conn_s[group].at[pl.ds(0, size)],
                 copied.at[group],
             )
@@ -140,53 +142,56 @@
         wide = low_half(piece.shape)
         full[begin : begin + half, :] = jnp.where(wide, piece, other)
         full[begin + half : begin + 2 * half, :] = jnp.where(wide, other, piece)
-    tail = rows - rows % 8
-    work[:, tail:, :] = jnp.zeros((pairs, work.shape[1] - tail, LANES), jnp.float32)
+    zero = jnp.zeros((8, LANES), jnp.float32)
+
+    @pl.loop(0, full.shape[0] // 64)
+    def _(n):
+        for bank in banks:
+            for r in range(0, 64, 8):
+                bank[pl.ds(pl.multiple_of(n * 64 + r, 8), 8), :] = zero
+
+    for buffer in inputs + terms:
+        buffer[...] = jnp.zeros_like(buffer)
     for copy in copies:
         copy.wait()
 
-    zero = jnp.zeros((8, LANES), jnp.float32)
-    share = full.shape[0] // pairs
-
-    @pl.loop(0, pairs)
-    def _(pair):
-        for j in range(rows):
-            low = full[pl.ds(conn_s[j // 8][j % 8, pair], 1), :]
-            high = full[pl.ds(conn_s[j // 8][j % 8, pairs + pair], 1), :]
-            work[pair, j : j + 1, :] = jnp.where(mask, low, high)
-        for bank in banks:
-            for r in range(0, share, 8):
-                bank[pl.ds(pl.multiple_of(pair * share + r, 8), 8), :] = zero
-
     big = mat[...].astype(jnp.bfloat16)
     small = (mat[...] - big.astype(jnp.float32)).astype(jnp.bfloat16)
-    step = 4
-
-    def weight(pair):
+
+    def index(j, pair, side):
+        return pl.ds(conn_s[j // GROUP][j % GROUP, side * pairs + pair], 1)
+
+    def gather(pair, into):
+        for j in range(rows):
+            low = full[index(j, pair, 0), :]
+            high = full[index(j, pair, 1), :]
+            into[j : j + 1, :] = jnp.where(mask, low, high)
+
+    def multiply(pair, source, into):
         low = jnp.where(pair < count_s[0], scale_s[pair], 0.0)
         high = jnp.where(pairs + pair < count_s[0], scale_s[pairs + pair], 0.0)
-        return jnp.where(mask, low, high)
-
-    @pl.loop(0, pairs // step)
-    def _(n):
-        piece = jnp.concatenate(
-            [work[n * step + k] * weight(n * step + k) for k in range(step)], axis=1
-        )
+        piece = source[...] * jnp.where(mask, low, high)
         high = piece.astype(jnp.bfloat16)
         low = (piece - high.astype(jnp.float32)).astype(jnp.bfloat16)
         dot = functools.partial(jnp.dot, preferred_element_type=jnp.float32)
-        piece = dot(big, high) + (dot(big, low) + dot(small, high))
-        for k in range(step):
-            work[n * step + k] = piece[:, k * LANES : (k + 1) * LANES]
-
-    @pl.loop(0, pairs)
-    def _(pair):
+        into[...] = dot(big, high) + (dot(big, low) + dot(small, high))
+
+    def scatter(pair, source):
         for i in range(rows):
-            term = work[pair, i : i + 1, :]
+            term = source[i : i + 1, :]
             for side in range(2):
                 bank = banks[(2 * i + side) % len(banks)]
-                at = pl.ds(conn_s[i // 8][i % 8, side * pairs + pair], 1)
+                at = index(i, pair, side)
                 bank[at, :] = bank[at, :] + term
+
+    @pl.loop(0, pairs // 2 + 1)
+    def _(n):
+        for odd in range(2):
+            pair = 2 * n + odd
+            before = jnp.maximum(pair - 1, 0)
+            scatter(jnp.maximum(pair - 2, 0), terms[odd])
+            multiply(jnp.minimum(before, pairs - 1), inputs[1 - odd], terms[1 - odd])
+            gather(jnp.minimum(pair, pairs - 1), inputs[odd])
 
     def summed(begin, size):
         at = pl.ds(begin, size)
@@ -271,7 +276,7 @@
     elems = elem_scale.shape[0]
     blocks, half = 3 * subs, cap // 2
     rows_up = (elem_matrix.shape[0] + 127) // 128 * 128
-    groups = -(-elem_matrix.shape[0] // 8)
+    groups = -(-elem_matrix.shape[0] // GROUP)
     f32 = jnp.float32
     params = pltpu.CompilerParams(vmem_limit_bytes=VMEM_LIMIT)
 
@@ -307,10 +312,10 @@
         scratch_shapes=[
             pltpu.VMEM((total, LANES), f32),
             pltpu.VMEM((rows_up, rows_up), f32),
-            pltpu.VMEM((elems // 2, rows_up, LANES), f32),
             pltpu.SemaphoreType.DMA((groups,)),
         ]
-        + [pltpu.SMEM((8, elems), jnp.int32)] * groups
+        + [pltpu.SMEM((GROUP, elems), jnp.int32)] * groups
+        + [pltpu.VMEM((rows_up, LANES), f32)] * 4
         + [pltpu.VMEM((total, LANES), f32)] * BANKS,
         compiler_params=params,
         name="element",

time: 149 us -> 135 us (0.906)
  Pallas kernels: 147 us -> 133 us
    pallas_call x2, Pallas kernels: 73.9 us -> 60.3 us  [on_device(): element(connectivity, elem_scale, elem_count, table, exchange(packed), el...]
where the time goes in v3:
time: 135 us
  Pallas kernels  133 us (99%)
    pallas_call x2, Pallas kernels, on_device(): element(connectivity, elem_scale, elem_count, table, exchange(packed), el...  60.3 us
    pallas_call x2, Pallas kernels, on_device(): exchange(packed)  26 us
    pallas_call x2, Pallas kernels, on_device(): exchange(partial)  25.9 us
    pallas_call x1, Pallas kernels, on_device(): pl.pallas_call(first_kernel, out_shape=(field_shape, table_shape, block_s...  9.45 us
    pallas_call x1, Pallas kernels, on_device(): pl.pallas_call(second_kernel, out_shape=field_shape, in_specs=[smem()] +...  6.98 us
    pallas_call x1, Pallas kernels, on_device(): pl.pallas_call(start_kernel, out_shape=(table_shape, block_shape), in_spe...  4.62 us

profile of v3, /device:TPU:3, one launch (start us, length us, event | category | flops | bytes accessed | tf_op | source)
XLA Modules:
  0.0 134.7 jit_solution(3064265048820216044)
XLA Ops:
  1.3 4.6 %start.1 = (f32[4104,128]{1,0:T(8,128)}, f32[12,64,128]{2,1,0:T(8,128)}) custom-call(s32[1,3,4,128]{3,2,1,0:T(4,128)} %owner_s.5, f32[64,4096]{1,0:T(8,128)} %older.1), custom_call_target="tpu_custom_call" | custom-call | tf_op jit(solution)/shard_map/start/pallas_call | solution.py:325
  5.9 13.7 %exchange.4.ghosts = f32[12,64,128]{2,1,0:T(8,128)} custom-call(f32[12,64,128]{2,1,0:T(8,128)} %get-tuple-element.12.send), custom_call_target="tpu_custom_call" | custom-call | tf_op jit(solution)/shard_map/exchange/pallas_call | solution.py:334
  19.6 30.2 %element.2 = (f32[4096,128]{1,0:T(8,128)}, f32[12,64,128]{2,1,0:T(8,128)}) custom-call(s32[125,128]{1,0:T(8,128)} %conn.3, f32[128]{0:T(128)} %scale_s.3, s32[1]{0:T(128)S(6)} %copy.10.count_s, f32[4104,128]{1,0:T(8,128)} %get-tuple-element.11.table, f32[12,64,128]{2,1,0:T(8,128)} %exchange.4.ghosts, f32[125,125]{1,0:T(8,128)} %matrix.3), custom_call_target="tpu_custom_call" | custom-call | tf_op jit(solution)/shard_map/element/pallas_call | solution.py:333
  49.7 13.6 %exchange.5.arrived = f32[12,64,128]{2,1,0:T(8,128)} custom-call(f32[12,64,128]{2,1,0:T(8,128)} %get-tuple-element.13.send), custom_call_target="tpu_custom_call" | custom-call | tf_op jit(solution)/shard_map/exchange/pallas_call | solution.py:344
  63.3 9.4 %first.1 = (f32[64,4096]{1,0:T(8,128)}, f32[4104,128]{1,0:T(8,128)}, f32[12,64,128]{2,1,0:T(8,128)}) custom-call(s32[1,3,4,128]{3,2,1,0:T(4,128)} %owner_s.5, f32[12,64,128]{2,1,0:T(8,128)} %exchange.5.arrived, f32[4096,128]{1,0:T(8,128)} %get-tuple-element.14.owned, f32[64,4096]{1,0:T(8,128)} %older.1, f32[1,4096]{1,0:T(1,128)} %bitcast.2, f32[1,4096]{1,0:T(1,128)} %bitcast.4), custom_call_target="tpu_custom_call" | custom-call | tf_op jit(solution)/shard_map/first/pallas_call | solution.py:336
  72.8 12.4 %exchange.6.ghosts = f32[12,64,128]{2,1,0:T(8,128)} custom-call(f32[12,64,128]{2,1,0:T(8,128)} %get-tuple-element.17.send), custom_call_target="tpu_custom_call" | custom-call | tf_op jit(solution)/shard_map/exchange/pallas_call | solution.py:346
  85.1 30.2 %element.3 = (f32[4096,128]{1,0:T(8,128)}, f32[12,64,128]{2,1,0:T(8,128)}) custom-call(s32[125,128]{1,0:T(8,128)} %conn.3, f32[128]{0:T(128)} %scale_s.3, s32[1]{0:T(128)S(6)} %copy.10.count_s, f32[4104,128]{1,0:T(8,128)} %get-tuple-element.16.table, f32[12,64,128]{2,1,0:T(8,128)} %exchange.6.ghosts, f32[125,125]{1,0:T(8,128)} %matrix.3), custom_call_target="tpu_custom_call" | custom-call | tf_op jit(solution)/shard_map/element/pallas_call | solution.py:345
  115.3 12.4 %exchange.7.arrived = f32[12,64,128]{2,1,0:T(8,128)} custom-call(f32[12,64,128]{2,1,0:T(8,128)} %get-tuple-element.18.send), custom_call_target="tpu_custom_call" | custom-call | tf_op jit(solution)/shard_map/exchange/pallas_call | solution.py:356
  127.7 7.0 %second.1 = f32[64,4096]{1,0:T(8,128)} custom-call(s32[1,3,4,128]{3,2,1,0:T(4,128)} %owner_s.5, f32[12,64,128]{2,1,0:T(8,128)} %exchange.7.arrived, f32[4096,128]{1,0:T(8,128)} %get-tuple-element.19.owned, f32[64,4096]{1,0:T(8,128)} %get-tuple-element.9.field, f32[64,4096]{1,0:T(8,128)} %older.1, f32[1,4096]{1,0:T(1,128)} %bitcast.3, f32[1,4096]{1,0:T(1,128)} %bitcast.5), custom_call_target="tpu_custom_call" | custom-call | tf_op jit(solution)/shard_map/second/pallas_call | solution.py:348
